TPU v7x, 256 devices: a whole 4x4x8 slice. The times are simulated.
256 devices in a mesh: row: 8 (over z), col: 32 (over y, x, core).
Axes of the slice: x: 4, y: 4, z: 8, core: 2. Of those that a mesh axis runs over, the one named last changes fastest.
Arguments:
- out_grads: bfloat16 [32, 48, 28672], P('col', None, 'row'), may hold values from -6 to 6
- acts: bfloat16 [32, 48, 8192], P('row', None, 'col'), may hold values from -6 to 6
- rot_out: bfloat16 [28672, 28672], P('row', 'col'), may hold values from -0.03125 to 0.03125
- rot_in: bfloat16 [8192, 8192], P('col', 'row'), may hold values from -0.0625 to 0.0625
- queries: bfloat16 [2, 28672, 8192], P(None, 'col', 'row'), may hold values from -0.00036621094 to 0.00036621094
- token_sequence: int32 [1024], replicated, may hold values from 0 to 31, never falling along the last dimension, each value on 1 to 48 neighbouring positions
Outputs:
- scores: float32 [1024, 2], P(('row', 'col'))
Inputs may be any that keep to these rules, and one draw needn't show every extreme that they name: `token_sequence`: values never fall along the tokens; every sequence 0 to 31 has 1 to 48 tokens, some sequence exactly 48; the k-th token of a sequence (from 0) sits in its slot k of out_grads and acts.
All inputs are finite; a program needn't handle non-finite values.
Results may differ from a plain program's by a relative error of at most 0.0041.
Values may be sent and summed in bfloat16 or wider, within the bound.
A program may use at most 128 MiB of HBM per device.

v0:
```python
import jax
import jax.numpy as jnp
from jax import lax
from jax.sharding import Mesh
from jax.sharding import PartitionSpec as P

COL = ("col_0", "col_1", "col_2")
ROW_COL = ("row", "col_0", "col_1", "col_2")


def copy_for_each(shard, axis):
    copies = jnp.broadcast_to(shard, (lax.axis_size(axis), *shard.shape))
    return lax.all_to_all(copies, axis, split_axis=0, concat_axis=0, tiled=True)


def laid_out(blocks, dim):
    lengths = list(blocks.shape[1:])
    lengths[dim] *= blocks.shape[0]
    return jnp.moveaxis(blocks, 0, dim).reshape(lengths)


def gathered_copies(shard, axis, dim):
    blocks = copy_for_each(shard, axis)
    return laid_out(blocks, dim)


def in_blocks(shard, dim, devices):
    lengths = shard.shape
    blocks = shard.reshape(*lengths[:dim], devices, lengths[dim] // devices, *lengths[dim + 1 :])
    return jnp.moveaxis(blocks, dim, 0)


def summed_on_arrival(shard, axis, dim):
    devices = lax.axis_size(axis)
    blocks = lax.all_to_all(in_blocks(shard, dim, devices), axis, 0, 0, tiled=True)
    return jnp.sum(blocks, axis=0)


def sum_by_chip_2(shard, chips, core, dim):
    sizes = (lax.axis_size(chips), lax.axis_size(core))
    blocks = in_blocks(shard, dim, sizes[0] * sizes[1])
    inside = blocks.shape[1:]
    blocks = blocks.reshape(*sizes, *inside).swapaxes(0, 1).reshape(-1, *inside)
    blocks = lax.psum_scatter(blocks, core, scatter_dimension=0, tiled=True)
    return lax.psum_scatter(blocks, chips, scatter_dimension=0, tiled=True)[0]


def token_places(token_sequence, seq_count, slot_count):
    token_count = token_sequence.shape[0]
    labels = jnp.arange(seq_count, dtype=jnp.int32)
    before = (token_sequence[:, None] < labels[None, :]).astype(jnp.int32)
    starts = jnp.sum(before, axis=0)
    member = (token_sequence[:, None] == labels[None, :]).astype(jnp.int32)
    own_start = jnp.sum(member * starts[None, :], axis=1)
    position = jnp.arange(token_count, dtype=jnp.int32) - own_start
    return token_sequence * slot_count + position


def local(out_grads, acts, rot_out, rot_in, queries, token_sequence):
    slot_count = out_grads.shape[1]
    seq_count = out_grads.shape[0] * lax.axis_size(COL)
    flat_index = token_places(token_sequence, seq_count, slot_count)
    act_slots = gathered_copies(acts, "row", 0)
    act_rows = jnp.take(
        act_slots.reshape(seq_count * slot_count, act_slots.shape[2]), flat_index, axis=0
    )
    piece = lax.all_gather(out_grads, COL, axis=0, tiled=True)
    flattened = piece.reshape(piece.shape[0] * piece.shape[1], piece.shape[2])
    slot_terms = jnp.dot(flattened, rot_out, preferred_element_type=jnp.float32)
    grad_terms = jnp.take(slot_terms, flat_index, axis=0)
    grad_share = summed_on_arrival(grad_terms, "row", 0).astype(jnp.bfloat16)
    rot_grads = gathered_copies(grad_share, "row", 0)
    act_share = sum_by_chip_2(
        jnp.dot(act_rows, rot_in, preferred_element_type=jnp.float32),
        ("col_0", "col_1"),
        "col_2",
        0,
    ).astype(jnp.bfloat16)
    rot_acts = gathered_copies(act_share, COL, 0)
    projected = jnp.einsum("tj,qij->tqi", rot_acts, queries, preferred_element_type=jnp.float32)
    score_terms = jnp.sum(projected * rot_grads[:, None, :], axis=2)
    return lax.psum_scatter(score_terms, ROW_COL, scatter_dimension=0, tiled=True)


def solution(mesh):
    torus = Mesh(
        mesh.devices.reshape(mesh.shape["row"], 4, 4, 2), ("row", "col_0", "col_1", "col_2")
    )
    in_specs = (
        P(COL, None, "row"),
        P("row", None, COL),
        P("row", COL),
        P(COL, "row"),
        P(None, COL, "row"),
        P(),
    )
    out_specs = P(ROW_COL, None)
    return jax.shard_map(local, mesh=torus, in_specs=in_specs, out_specs=out_specs, check_vma=False)
```

profile of v0, /device:TPU:1, one launch (start us, length us, event | category | flops | bytes accessed | tf_op | source)
XLA Modules:
  0.0 380.5 jit_solution(10519326108349929063)
XLA Ops:
  7.4 0.7 all-gather.2.cloned.1.call-update
  8.1 1.9 broadcast_in_dim.39
  9.9 9.0 %all-to-all-start = ((bf16[8,4,48,256]{3,2,1,0:T(8,128)(2,1)}), bf16[8,4,48,256]{3,2,1,0:T(8,128)(2,1)S(1)}, u32[]{:S(2)}, u32[]{:S(2)}) async-start(bf16[8,4,48,256]{3,2,1,0:T(8,128)(2,1)} %broadcast_in_dim.39), calls=%async_computation | async-start | bytes 1572864 | tf_op jit(solution)/shard_map/all_to_all | solution.py:13
  19.0 0.8 convert_reduce_fusion
  19.8 0.8 select_reduce_fusion
  20.6 0.7 compare_and_fusion
  21.3 0.7 broadcast_clamp_fusion
  22.0 20.5 %all-to-all-done = bf16[8,4,48,256]{3,2,1,0:T(8,128)(2,1)S(1)} async-done(((bf16[8,4,48,256]{3,2,1,0:T(8,128)(2,1)}), bf16[8,4,48,256]{3,2,1,0:T(8,128)(2,1)S(1)}, u32[]{:S(2)}, u32[]{:S(2)}) %all-to-all-start) | async-done | bytes 786464 | tf_op jit(solution)/shard_map/all_to_all | solution.py:13
  42.5 3.9 %gather_fusion = bf16[1024,256]{1,0:T(8,128)(2,1)S(1)} fusion(bf16[1536,256]{1,0:T(8,128)(2,1)S(1)} %bitcast.24, s32[1024]{0:T(1024)S(1)} %broadcast_clamp_fusion), kind=kCustom, calls=%fused_computation | custom fusion | bytes 1052672 | tf_op jit(solution)/shard_map/jit(_take)/gather | solution.py:64
  46.5 0.8 fusion
  47.2 2.3 copy.14
  49.5 29.5 %all-gather.2.cloned.1.call-done = bf16[32,48,3584]{2,1,0:T(8,128)(2,1)} async-done(((bf16[1,48,3584]{2,1,0:T(8,128)(2,1)}), bf16[32,48,3584]{2,1,0:T(8,128)(2,1)}) %all-gather.2.cloned.1.call-update) | async-done | bytes 11010064 | tf_op jit(solution)/shard_map/all_gather | solution.py:67
  79.1 17.0 %fusion.5 = f32[1536,896]{1,0:T(8,128)} fusion(bf16[1536,3584]{1,0:T(8,128)(2,1)} %bitcast.29, bf16[3584,896]{1,0:T(8,128)(2,1)} %param.8), kind=kOutput, calls=%fused_computation.19 | convolution fusion | flops 9865003008 | bytes 22937600 | tf_op jit(solution)/shard_map/dot_general | solution.py:69
  96.1 8.6 %gather_fusion.1 = f32[1024,896]{1,0:T(8,128)} fusion(f32[1536,896]{1,0:T(8,128)} %fusion.5, s32[1024]{0:T(1024)S(1)} %broadcast_clamp_fusion), kind=kCustom, calls=%fused_computation.1 | custom fusion | bytes 7344128 | tf_op jit(solution)/shard_map/jit(_take)/gather | solution.py:70
  104.7 4.2 %broadcast_select_fusion = f32[8,128,896]{2,1,0:T(8,128)} fusion(f32[8,128,896]{2,1,0:T(8,128)} %bitcast.27, pred[8,128]{1,0:T(8,128)(4,1)S(1)} %bitcast.28), kind=kLoop, calls=%fused_computation.4 | loop fusion | flops 917504 | bytes 7341056 | tf_op jit(solution)/shard_map/jit(_take)/select_n | solution.py:70
  108.9 6.7 %all-to-all-start.2 = ((f32[8,128,896]{2,1,0:T(8,128)}), f32[8,128,896]{2,1,0:T(8,128)}, u32[]{:S(2)}, u32[]{:S(2)}) async-start(f32[8,128,896]{2,1,0:T(8,128)} %broadcast_select_fusion), calls=%async_computation.3 | async-start | bytes 7340032 | tf_op jit(solution)/shard_map/all_to_all | solution.py:35
  115.7 0.5 reduce-scatter.8.cloned.1.call-update
  116.2 85.0 %all-to-all-done.2 = f32[8,128,896]{2,1,0:T(8,128)} async-done(((f32[8,128,896]{2,1,0:T(8,128)}), f32[8,128,896]{2,1,0:T(8,128)}, u32[]{:S(2)}, u32[]{:S(2)}) %all-to-all-start.2) | async-done | bytes 3670048 | tf_op jit(solution)/shard_map/all_to_all | solution.py:35
  201.2 2.2 reduce_sum.38
  203.7 1.5 broadcast_in_dim.46
  205.1 3.6 all-to-all-start.3
  208.8 0.9 convert_bitcast_fusion
  209.7 42.1 %all-to-all-done.3 = bf16[8,128,896]{1,2,0:T(8,128)(2,1)S(1)} async-done(((bf16[8,128,896]{1,2,0:T(8,128)(2,1)}), bf16[8,128,896]{1,2,0:T(8,128)(2,1)S(1)}, u32[]{:S(2)}, u32[]{:S(2)}) %all-to-all-start.3) | async-done | bytes 1835040 | tf_op jit(solution)/shard_map/all_to_all | solution.py:13
  251.8 1.6 broadcast_in_dim.42
  253.4 8.6 %all-to-all-start.1 = ((bf16[32,32,1024]{2,1,0:T(8,128)(2,1)}), bf16[32,32,1024]{2,1,0:T(8,128)(2,1)}, u32[]{:S(2)}, u32[]{:S(2)}) async-start(bf16[32,32,1024]{2,1,0:T(8,128)(2,1)} %broadcast_in_dim.42), calls=%async_computation.2 | async-start | bytes 4194304 | tf_op jit(solution)/shard_map/all_to_all | solution.py:13
  262.0 2.7 copy.16
  264.7 3.6 bitcast_convert_fusion
  268.3 5.0 %copy.17 = f32[1024,896]{0,1:T(8,128)} copy(f32[1024,896]{1,0:T(8,128)} %bitcast_convert_fusion) | data formatting | bytes 7340032 | tf_op jit(solution)/shard_map/convert_element_type | solution.py:81
  273.3 16.6 %all-to-all-done.1 = bf16[32,32,1024]{2,1,0:T(8,128)(2,1)} async-done(((bf16[32,32,1024]{2,1,0:T(8,128)(2,1)}), bf16[32,32,1024]{2,1,0:T(8,128)(2,1)}, u32[]{:S(2)}, u32[]{:S(2)}) %all-to-all-start.1) | async-done | bytes 2097184 | tf_op jit(solution)/shard_map/all_to_all | solution.py:13
  289.9 7.8 %multiply_reduce_fusion = f32[1024,2]{0,1:T(2,128)S(1)} fusion(f32[1024,896]{0,1:T(8,128)} %copy.17, bf16[1024,1024,1]{1,0,2:T(8,128)(2,1)} %bitcast.6, bf16[2,896,1024]{2,1,0:T(8,128)(2,1)} %param.10), kind=kOutput, calls=%fused_computation.2 | convolution fusion | flops 3761764352 | bytes 9445376 | tf_op jit(solution)/shard_map/tj,qij->tqi/dot_general | solution.py:80
  297.8 74.6 %all-reduce.1 = f32[1024,2]{0,1:T(2,128)S(1)} all-reduce(f32[1024,2]{0,1:T(2,128)S(1)} %multiply_reduce_fusion), channel_id=4, replica_groups=mesh['row'=8,'col_0'=4,'col_1'=4,'col_2'=2] {'row','col_0','col_1','col_2'}, use_global_device_ids=true, to_apply=%region_6.7.clone | all-reduce | flops 2048 | bytes 16384
  372.4 0.6 constant_dynamic-slice_fusion
  (11 shorter events, 0.3 us)
Async XLA Ops:
  7.4 39.1 %copy-start = (bf16[256,1024]{1,0:T(8,128)(2,1)S(1)}, bf16[256,1024]{1,0:T(8,128)(2,1)}, u32[]{:S(2)}) copy-start(bf16[256,1024]{1,0:T(8,128)(2,1)} %param.9) | copy-start | bytes 1572868
  7.4 71.7 %all-gather.2.cloned.1.call-start = ((), (), s32[]{:S(2)}) async-start(), calls=%async_computation.7 | async-start | bytes 11354112 | tf_op jit(solution)/shard_map/all_gather | solution.py:67
  9.9 32.6 %all-to-all-start = ((bf16[8,4,48,256]{3,2,1,0:T(8,128)(2,1)}), bf16[8,4,48,256]{3,2,1,0:T(8,128)(2,1)S(1)}, u32[]{:S(2)}, u32[]{:S(2)}) async-start(bf16[8,4,48,256]{3,2,1,0:T(8,128)(2,1)} %broadcast_in_dim.39), calls=%async_computation | async-start | bytes 1572864 | tf_op jit(solution)/shard_map/all_to_all | solution.py:13
  19.0 96.7 %reduce-scatter.6.cloned.1.call-start = ((), (), s32[]{:S(2)}) async-start(), calls=%async_computation.6 | async-start | bytes 6291456 | tf_op jit(solution)/shard_map/reduce_scatter | solution.py:44
  108.9 92.4 %all-to-all-start.2 = ((f32[8,128,896]{2,1,0:T(8,128)}), f32[8,128,896]{2,1,0:T(8,128)}, u32[]{:S(2)}, u32[]{:S(2)}) async-start(f32[8,128,896]{2,1,0:T(8,128)} %broadcast_select_fusion), calls=%async_computation.3 | async-start | bytes 7340032 | tf_op jit(solution)/shard_map/all_to_all | solution.py:35
  115.6 93.1 %reduce-scatter.8.cloned.1.call-start = ((), (), s32[]{:S(2)}) async-start(), calls=%async_computation.8 | async-start | bytes 2228224
  205.1 46.7 %all-to-all-start.3 = ((bf16[8,128,896]{1,2,0:T(8,128)(2,1)}), bf16[8,128,896]{1,2,0:T(8,128)(2,1)S(1)}, u32[]{:S(2)}, u32[]{:S(2)}) async-start(bf16[8,128,896]{1,2,0:T(8,128)(2,1)} %broadcast_in_dim.46), calls=%async_computation.4 | async-start | bytes 3670016 | tf_op jit(solution)/shard_map/all_to_all | solution.py:13
  253.4 36.5 %all-to-all-start.1 = ((bf16[32,32,1024]{2,1,0:T(8,128)(2,1)}), bf16[32,32,1024]{2,1,0:T(8,128)(2,1)}, u32[]{:S(2)}, u32[]{:S(2)}) async-start(bf16[32,32,1024]{2,1,0:T(8,128)(2,1)} %broadcast_in_dim.42), calls=%async_computation.2 | async-start | bytes 4194304 | tf_op jit(solution)/shard_map/all_to_all | solution.py:13
  289.9 83.1 %copy-start.1 = (bf16[256,1024]{1,0:T(8,128)(2,1)S(1)}, bf16[256,1024]{1,0:T(8,128)(2,1)}, u32[]{:S(2)}) copy-start(bf16[256,1024]{1,0:T(8,128)(2,1)} %param.9) | copy-start | bytes 1572868
Sparse Core Ops, SparseCore 0:
  10.7 68.2 all-gather.1
Sparse Core Ops, SparseCore 1:
  49.6 14.1 reduce-scatter.5
  120.1 77.6 reduce-scatter.7
where the time goes:
time: 381 us; the launch traced here: 380 us
  waiting for transfers between devices  195 us (51%)
  blocking collectives  74.6 us (20%)
  local copies, waits for them, and re-layouts  28.3 us (7%)
  starting transfers between devices  28 us (7%)
  matrix products  25.6 us (7%)
  between operations  14.9 us (4%)
  other arithmetic  13.8 us (4%)
    all_to_all x1, waiting for transfers between devices, summed_on_arrival(): lax.all_to_all(in_blocks(shard, dim, devices), axis, 0, 0, tiled=True)  85 us
    all_to_all x3, waiting for transfers between devices, copy_for_each(): return lax.all_to_all(copies, axis, split_axis=0, concat_axis=0, tiled=True)  79.3 us
    unnamed x1, blocking collectives  74.6 us
    all_gather x1, waiting for transfers between devices, local(): piece = lax.all_gather(out_grads, COL, axis=0, tiled=True)  29.5 us
    all_to_all x3, starting transfers between devices, copy_for_each(): return lax.all_to_all(copies, axis, split_axis=0, concat_axis=0, tiled=True)  21.2 us
    dot_general x1, matrix products, local(): slot_terms = jnp.dot(flattened, rot_out, preferred_element_type=jnp.float32)  17 us
    gather x1, local copies, waits for them, and re-layouts, local(): grad_terms = jnp.take(slot_terms, flat_index, axis=0)  8.63 us
    dot_general x1, matrix products, local(): jnp.einsum('tj,qij->tqi', rot_acts, queries, preferred_element_type=jnp.f...  7.84 us
  transfers between devices with their start and end apart: 7, of which 5 were waited for; matrix products, arithmetic and copies ran while one was open for 15% of the time, Pallas kernels for 0%

commit v1 on v0

--- a/solution.py
+++ b/solution.py
@@ -6,6 +6,13 @@
 
 COL = ("col_0", "col_1", "col_2")
 ROW_COL = ("row", "col_0", "col_1", "col_2")
+
+
+def all_by_exchange(x, axis, along):
+    size = lax.axis_size(axis)
+    blocks = jnp.stack([x for _ in range(size)])
+    blocks = lax.all_to_all(blocks, axis, split_axis=0, concat_axis=0)
+    return jnp.concatenate(blocks, axis=along)
 
 
 def copy_for_each(shard, axis):
@@ -64,7 +71,7 @@
     act_rows = jnp.take(
         act_slots.reshape(seq_count * slot_count, act_slots.shape[2]), flat_index, axis=0
     )
-    piece = lax.all_gather(out_grads, COL, axis=0, tiled=True)
+    piece = all_by_exchange(out_grads, COL, 0)
     flattened = piece.reshape(piece.shape[0] * piece.shape[1], piece.shape[2])
     slot_terms = jnp.dot(flattened, rot_out, preferred_element_type=jnp.float32)
     grad_terms = jnp.take(slot_terms, flat_index, axis=0)

time: 381 us -> 486 us (1.28)
  waiting for transfers between devices: 195 us -> 260 us
  blocking collectives: 74.6 us -> 105 us
  starting transfers between devices: 28 us -> 36.4 us
  local copies, waits for them, and re-layouts: 28.3 us -> 33.8 us
    all_to_all x0 -> x1, waiting for transfers between devices: none -> 125 us  [all_by_exchange(): blocks = lax.all_to_all(blocks, axis, split_axis=0, concat_axis=0)]
    all_to_all x0 -> x1, blocking collectives: none -> 30.4 us  [copy_for_each(): return lax.all_to_all(copies, axis, split_axis=0, concat_axis=0, tiled=True)]
    all_gather x1 -> x0, waiting for transfers between devices: 29.5 us -> none  [local(): piece = lax.all_gather(out_grads, COL, axis=0, tiled=True)]
    all_to_all x3 -> x2, waiting for transfers between devices: 79.3 us -> 58.5 us  [copy_for_each(): return lax.all_to_all(copies, axis, split_axis=0, concat_axis=0, tiled=True)]
    all_to_all x0 -> x1, starting transfers between devices: none -> 9.72 us  [all_by_exchange(): blocks = lax.all_to_all(blocks, axis, split_axis=0, concat_axis=0)]
    all_to_all x1, waiting for transfers between devices: 85 us -> 75.9 us  [summed_on_arrival(): lax.all_to_all(in_blocks(shard, dim, devices), axis, 0, 0, tiled=True)]
    another operation x0 -> x1, local copies, waits for them, and re-layouts: none -> 6.25 us  [all_by_exchange(): blocks = jnp.stack([x for _ in range(size)])]
    all_to_all x3 -> x2, starting transfers between devices: 21.2 us -> 22.1 us  [copy_for_each(): return lax.all_to_all(copies, axis, split_axis=0, concat_axis=0, tiled=True)]
  transfers between devices with their start and end apart: 7 -> 6, of which waited for: 5 -> 4; matrix products, arithmetic and copies ran while one was open for 15% -> 11% of each run, Pallas kernels for 0% -> 0%
where the time goes in v1:
time: 486 us
  waiting for transfers between devices  260 us (53%)
  blocking collectives  105 us (22%)
  starting transfers between devices  36.4 us (7%)
  local copies, waits for them, and re-layouts  33.8 us (7%)
  matrix products  25.6 us (5%)
  between operations  13.5 us (3%)
  other arithmetic  11.1 us (2%)
    all_to_all x1, waiting for transfers between devices, all_by_exchange(): blocks = lax.all_to_all(blocks, axis, split_axis=0, concat_axis=0)  125 us
    all_to_all x1, waiting for transfers between devices, summed_on_arrival(): lax.all_to_all(in_blocks(shard, dim, devices), axis, 0, 0, tiled=True)  75.9 us
    unnamed x1, blocking collectives  74.5 us
    all_to_all x2, waiting for transfers between devices, copy_for_each(): return lax.all_to_all(copies, axis, split_axis=0, concat_axis=0, tiled=True)  58.5 us
    all_to_all x1, blocking collectives, copy_for_each(): return lax.all_to_all(copies, axis, split_axis=0, concat_axis=0, tiled=True)  30.4 us
    all_to_all x2, starting transfers between devices, copy_for_each(): return lax.all_to_all(copies, axis, split_axis=0, concat_axis=0, tiled=True)  22.1 us
    dot_general x1, matrix products, local(): slot_terms = jnp.dot(flattened, rot_out, preferred_element_type=jnp.float32)  17 us
  transfers between devices with their start and end apart: 6, of which 4 were waited for; matrix products, arithmetic and copies ran while one was open for 11% of the time, Pallas kernels for 0%

profile of v1, /device:TPU:1, one launch (start us, length us, event | category | flops | bytes accessed | tf_op | source)
XLA Modules:
  0.0 485.6 jit_solution(9007129825620013311)
XLA Ops:
  6.5 1.0 broadcast_in_dim.39
  7.6 30.4 %all_to_all.25 = bf16[8,4,48,256]{3,2,1,0:T(8,128)(2,1)S(1)} all-to-all(bf16[8,4,48,256]{3,2,1,0:T(8,128)(2,1)S(1)} %broadcast_in_dim.39), channel_id=1, replica_groups=mesh['row'=8,'col_0'=4,'col_1'=4,'col_2'=2] {'row'}, dimensions={0} | all-to-all | bytes 1572864 | tf_op jit(solution)/shard_map/all_to_all | solution.py:20
  38.0 6.3 %stack.2 = bf16[32,1,48,3584]{3,2,1,0:T(8,128)(2,1)} broadcast(bf16[48,3584]{1,0:T(8,128)(2,1)} %bitcast.29), dimensions={2,3} | broadcast | bytes 11354112 | tf_op jit(solution)/shard_map/stack | solution.py:13
  44.2 9.7 %all-to-all-start.2 = ((bf16[32,1,48,3584]{3,2,1,0:T(8,128)(2,1)}), bf16[32,1,48,3584]{3,2,1,0:T(8,128)(2,1)}, u32[]{:S(2)}, u32[]{:S(2)}) async-start(bf16[32,1,48,3584]{3,2,1,0:T(8,128)(2,1)} %stack.2), calls=%async_computation.3 | async-start | bytes 22020096 | tf_op jit(solution)/shard_map/all_to_all | solution.py:14
  54.0 0.1 convert_reduce_fusion
  54.1 0.1 select_reduce_fusion
  54.3 3.9 gather_fusion
  58.2 0.8 fusion
  59.0 2.3 copy.14
  61.3 125.1 %all-to-all-done.2 = bf16[32,1,48,3584]{3,2,1,0:T(8,128)(2,1)} async-done(((bf16[32,1,48,3584]{3,2,1,0:T(8,128)(2,1)}), bf16[32,1,48,3584]{3,2,1,0:T(8,128)(2,1)}, u32[]{:S(2)}, u32[]{:S(2)}) %all-to-all-start.2) | async-done | bytes 11010080 | tf_op jit(solution)/shard_map/all_to_all | solution.py:14
  186.4 17.0 %fusion.5 = f32[1536,896]{1,0:T(8,128)} fusion(bf16[1536,3584]{1,0:T(8,128)(2,1)} %bitcast.9, bf16[3584,896]{1,0:T(8,128)(2,1)} %param.8), kind=kOutput, calls=%fused_computation.19 | convolution fusion | flops 9865003008 | bytes 22937600 | tf_op jit(solution)/shard_map/dot_general | solution.py:76
  203.5 8.6 %gather_fusion.1 = f32[1024,896]{1,0:T(8,128)} fusion(f32[1536,896]{1,0:T(8,128)} %fusion.5, s32[1024]{0:T(1024)S(1)} %broadcast_clamp_fusion), kind=kCustom, calls=%fused_computation.1 | custom fusion | bytes 7344128 | tf_op jit(solution)/shard_map/jit(_take)/gather | solution.py:77
  212.1 4.2 broadcast_select_fusion
  216.3 4.5 all-to-all-start.3
  220.8 0.0 reduce-scatter.8.cloned.1.call-start
  220.9 0.7 reduce-scatter.8.cloned.1.call-update
  221.5 75.9 %all-to-all-done.3 = f32[8,128,896]{2,1,0:T(8,128)} async-done(((f32[8,128,896]{2,1,0:T(8,128)}), f32[8,128,896]{2,1,0:T(8,128)}, u32[]{:S(2)}, u32[]{:S(2)}) %all-to-all-start.3) | async-done | bytes 3670048 | tf_op jit(solution)/shard_map/all_to_all | solution.py:42
  297.5 2.2 reduce_sum.38
  299.7 0.2 copy.15
  299.9 1.5 broadcast_in_dim.46
  301.4 9.0 %all-to-all-start.4 = ((bf16[8,128,896]{1,2,0:T(8,128)(2,1)}), bf16[8,128,896]{1,2,0:T(8,128)(2,1)S(1)}, u32[]{:S(2)}, u32[]{:S(2)}) async-start(bf16[8,128,896]{1,2,0:T(8,128)(2,1)} %broadcast_in_dim.46), calls=%async_computation.5 | async-start | bytes 3670016 | tf_op jit(solution)/shard_map/all_to_all | solution.py:20
  310.4 0.9 convert_bitcast_fusion
  311.3 42.0 %all-to-all-done.4 = bf16[8,128,896]{1,2,0:T(8,128)(2,1)S(1)} async-done(((bf16[8,128,896]{1,2,0:T(8,128)(2,1)}), bf16[8,128,896]{1,2,0:T(8,128)(2,1)S(1)}, u32[]{:S(2)}, u32[]{:S(2)}) %all-to-all-start.4) | async-done | bytes 1835040 | tf_op jit(solution)/shard_map/all_to_all | solution.py:20
  353.3 1.6 broadcast_in_dim.42
  354.9 13.1 %all-to-all-start.1 = ((bf16[32,32,1024]{2,1,0:T(8,128)(2,1)}), bf16[32,32,1024]{2,1,0:T(8,128)(2,1)}, u32[]{:S(2)}, u32[]{:S(2)}) async-start(bf16[32,32,1024]{2,1,0:T(8,128)(2,1)} %broadcast_in_dim.42), calls=%async_computation.2 | async-start | bytes 4194304 | tf_op jit(solution)/shard_map/all_to_all | solution.py:20
  368.0 2.7 copy.16
  370.7 3.6 bitcast_convert_fusion
  374.3 5.0 %copy.17 = f32[1024,896]{0,1:T(8,128)} copy(f32[1024,896]{1,0:T(8,128)} %bitcast_convert_fusion) | data formatting | bytes 7340032 | tf_op jit(solution)/shard_map/convert_element_type | solution.py:88
  379.3 16.5 %all-to-all-done.1 = bf16[32,32,1024]{2,1,0:T(8,128)(2,1)} async-done(((bf16[32,32,1024]{2,1,0:T(8,128)(2,1)}), bf16[32,32,1024]{2,1,0:T(8,128)(2,1)}, u32[]{:S(2)}, u32[]{:S(2)}) %all-to-all-start.1) | async-done | bytes 2097184 | tf_op jit(solution)/shard_map/all_to_all | solution.py:20
  395.8 7.8 %multiply_reduce_fusion = f32[1024,2]{0,1:T(2,128)S(1)} fusion(f32[1024,896]{0,1:T(8,128)} %copy.17, bf16[1024,1024,1]{1,0,2:T(8,128)(2,1)} %bitcast.6, bf16[2,896,1024]{2,1,0:T(8,128)(2,1)} %param.10), kind=kOutput, calls=%fused_computation.2 | convolution fusion | flops 3761764352 | bytes 9445376 | tf_op jit(solution)/shard_map/tj,qij->tqi/dot_general | solution.py:87
  403.7 74.5 %all-reduce.1 = f32[1024,2]{0,1:T(2,128)S(1)} all-reduce(f32[1024,2]{0,1:T(2,128)S(1)} %multiply_reduce_fusion), channel_id=4, replica_groups=mesh['row'=8,'col_0'=4,'col_1'=4,'col_2'=2] {'row','col_0','col_1','col_2'}, use_global_device_ids=true, to_apply=%region_6.7.clone | all-reduce | flops 2048 | bytes 16384
  478.2 0.6 constant_dynamic-slice_fusion
  (12 shorter events, 0.1 us)
Async XLA Ops:
  6.5 51.7 %copy-start = (bf16[256,1024]{1,0:T(8,128)(2,1)S(1)}, bf16[256,1024]{1,0:T(8,128)(2,1)}, u32[]{:S(2)}) copy-start(bf16[256,1024]{1,0:T(8,128)(2,1)} %param.9) | copy-start | bytes 1572868
  44.2 9.8 %copy-start.2 = (s32[1024]{0:T(1024)S(1)}, s32[1024]{0:T(1024)}, u32[]{:S(2)}) copy-start(s32[1024]{0:T(1024)} %param.11) | copy-start | bytes 12292
  44.2 142.2 %all-to-all-start.2 = ((bf16[32,1,48,3584]{3,2,1,0:T(8,128)(2,1)}), bf16[32,1,48,3584]{3,2,1,0:T(8,128)(2,1)}, u32[]{:S(2)}, u32[]{:S(2)}) async-start(bf16[32,1,48,3584]{3,2,1,0:T(8,128)(2,1)} %stack.2), calls=%async_computation.3 | async-start | bytes 22020096 | tf_op jit(solution)/shard_map/all_to_all | solution.py:14
  54.0 166.9 %reduce-scatter.6.cloned.1.call-start = ((), (), s32[]{:S(2)}) async-start(), calls=%async_computation.7 | async-start | bytes 6291456 | tf_op jit(solution)/shard_map/reduce_scatter | solution.py:51
  216.3 81.2 %all-to-all-start.3 = ((f32[8,128,896]{2,1,0:T(8,128)}), f32[8,128,896]{2,1,0:T(8,128)}, u32[]{:S(2)}, u32[]{:S(2)}) async-start(f32[8,128,896]{2,1,0:T(8,128)} %broadcast_select_fusion), calls=%async_computation.4 | async-start | bytes 7340032 | tf_op jit(solution)/shard_map/all_to_all | solution.py:42
  220.8 89.6 %reduce-scatter.8.cloned.1.call-start = ((), (), s32[]{:S(2)}) async-start(), calls=%async_computation.8 | async-start | bytes 2228224
  301.4 52.0 %all-to-all-start.4 = ((bf16[8,128,896]{1,2,0:T(8,128)(2,1)}), bf16[8,128,896]{1,2,0:T(8,128)(2,1)S(1)}, u32[]{:S(2)}, u32[]{:S(2)}) async-start(bf16[8,128,896]{1,2,0:T(8,128)(2,1)} %broadcast_in_dim.46), calls=%async_computation.5 | async-start | bytes 3670016 | tf_op jit(solution)/shard_map/all_to_all | solution.py:20
  354.9 40.9 %all-to-all-start.1 = ((bf16[32,32,1024]{2,1,0:T(8,128)(2,1)}), bf16[32,32,1024]{2,1,0:T(8,128)(2,1)}, u32[]{:S(2)}, u32[]{:S(2)}) async-start(bf16[32,32,1024]{2,1,0:T(8,128)(2,1)} %broadcast_in_dim.42), calls=%async_computation.2 | async-start | bytes 4194304 | tf_op jit(solution)/shard_map/all_to_all | solution.py:20
  395.8 83.0 %copy-start.1 = (bf16[256,1024]{1,0:T(8,128)(2,1)S(1)}, bf16[256,1024]{1,0:T(8,128)(2,1)}, u32[]{:S(2)}) copy-start(bf16[256,1024]{1,0:T(8,128)(2,1)} %param.9) | copy-start | bytes 1572868
Sparse Core Ops, SparseCore 0:
  61.5 13.9 reduce-scatter.5
  225.6 82.0 reduce-scatter.7
